TPU v7x, 32 devices: a whole 2x2x4 slice. The times are simulated.
32 devices in a mesh: row: 4 (over y, core), col: 8 (over z, x).
Axes of the slice: x: 2, y: 2, z: 4, core: 2. Of those that a mesh axis runs over, the one named last changes fastest.
Arguments:
- points: float32 [3, 4, 8192], P(None, None, ('row', 'col')), may hold values from 0 to 1
- weights: float32 [4, 8192], P(None, ('row', 'col')), may hold values from 0.05 to 0.2
- shift: float32 [8192], P(('row', 'col')), may hold values from 0.5 to 4
- cluster_rank: int32 [16], replicated, may hold values from 0 to 15, each once
Outputs:
- factor: float32 [4, 4, 512, 2, 8, 512], P(None, 'row', None, None, 'col')
Inputs may be any that keep to these rules, and one draw needn't show every extreme that they name: `cluster_rank`: every cluster has a distinct elimination position.
All inputs are finite; a program needn't handle non-finite values.
Results may differ from a plain program's by a relative error of at most 0.0003.
Values sent between devices are 32-bit elements; how exact they have to be, the bound alone decides.
A program may use at most 128 MiB of HBM per device.

v0:
```python
import jax
import jax.numpy as jnp
from jax import lax
from jax.sharding import PartitionSpec as P

SOFTENING_SQUARED = 0.0004


def broadcast(value, axis, source):
    kept = jnp.where(lax.axis_index(axis) == source, value, 0).astype(value.dtype)
    return lax.psum(kept, axis)


def kernel_block(row_geometry, col_geometry):
    values = jnp.zeros((row_geometry.shape[2], col_geometry.shape[2]), jnp.float32)
    for first in range(row_geometry.shape[1]):
        for second in range(col_geometry.shape[1]):
            squared = SOFTENING_SQUARED
            for coordinate in range(3):
                offset = (
                    row_geometry[coordinate, first][:, None]
                    - col_geometry[coordinate, second][None, :]
                )
                squared = squared + offset * offset
            product = row_geometry[3, first][:, None] * col_geometry[3, second][None, :]
            values = values + product * lax.rsqrt(squared)
    return values


def reorder(points, weights, shift, cluster_rank):
    clusters = cluster_rank.shape[0]
    positions = jnp.arange(clusters, dtype=jnp.int32)
    order = jnp.sum(
        jnp.where(cluster_rank[None, :] == positions[:, None], positions[None, :], 0), axis=1
    )
    geometry = jnp.concatenate([points, weights[None]], axis=0)
    quadrature = geometry.shape[1]
    geometry = geometry.reshape(4, quadrature, clusters, -1)
    geometry = jnp.take(geometry, order, axis=2).reshape(4, quadrature, -1)
    shifted = jnp.take(shift.reshape(clusters, -1), order, axis=0).reshape(-1)
    return (geometry, shifted)


def shards(points, weights, shift, cluster_rank):
    row_count = lax.axis_size("row")
    col_count = lax.axis_size("col")
    row_index = lax.axis_index("row")
    col_index = lax.axis_index("col")
    all_points, all_weights, all_shift = (
        lax.all_gather(points, ("row", "col"), axis=2, tiled=True),
        lax.all_gather(weights, ("row", "col"), axis=1, tiled=True),
        lax.all_gather(shift, ("row", "col"), axis=0, tiled=True),
    )
    geometry, shifted = reorder(all_points, all_weights, all_shift, cluster_rank)
    clusters = cluster_rank.shape[0]
    tile = shifted.shape[0] // clusters
    row_tiles = clusters // row_count
    col_tiles = clusters // col_count

    def assemble(row_start, col_start, row_length, col_length):
        rows = lax.dynamic_slice_in_dim(geometry, row_start, row_length, 2)
        columns = lax.dynamic_slice_in_dim(geometry, col_start, col_length, 2)
        values = kernel_block(rows, columns)
        row_ids = row_start + jnp.arange(row_length, dtype=jnp.int32)
        col_ids = col_start + jnp.arange(col_length, dtype=jnp.int32)
        row_shift = lax.dynamic_slice_in_dim(shifted, row_start, row_length, 0)
        return values + jnp.where(row_ids[:, None] == col_ids[None, :], row_shift[:, None], 0.0)

    stacked_rows = []
    for slot_row in range(row_tiles):
        block_row = slot_row * row_count + row_index
        tile_list = []
        for slot_col in range(col_tiles):
            block_col = slot_col * col_count + col_index
            tile_list.append(
                lax.cond(
                    block_row >= block_col,
                    lambda: assemble(block_row * tile, block_col * tile, tile, tile),
                    lambda: jnp.zeros((tile, tile), jnp.float32),
                )
            )
        stacked_rows.append(jnp.stack(tile_list, axis=1))
    tiles = jnp.stack(stacked_rows, axis=0)
    block_rows = jnp.arange(row_tiles, dtype=jnp.int32) * row_count + row_index
    block_cols = jnp.arange(col_tiles, dtype=jnp.int32) * col_count + col_index
    for step in range(2):
        diagonal_row = step % row_count
        diagonal_slot = step // row_count
        column_root = step % col_count
        column_slot = step // col_count
        diagonal = broadcast(tiles[diagonal_slot, :, column_slot, :], "row", diagonal_row)
        diagonal_factor = jnp.linalg.cholesky(diagonal)
        column = tiles[:, :, column_slot, :]
        repeated = jnp.broadcast_to(diagonal_factor, (row_tiles, tile, tile))
        solved = lax.linalg.triangular_solve(
            repeated, column, left_side=False, lower=True, transpose_a=True
        )
        below = (block_rows > step)[:, None, None]
        at_step = (block_rows == step)[:, None, None]
        panel = jnp.where(below, solved, jnp.where(at_step, diagonal_factor[None], column))
        tiles = tiles.at[:, :, column_slot, :].set(
            jnp.where(col_index == column_root, panel, column)
        )
        row_factors = broadcast(panel, "col", column_root)
        slots = (jnp.arange(col_tiles, dtype=jnp.int32) * col_count + col_index) // row_count
        candidates = jnp.take(row_factors, slots, axis=0)
        col_factors = broadcast(candidates, "row", col_index % row_count)
        product = jnp.einsum(
            "iab,jcb->iajc", row_factors, col_factors, precision=lax.Precision.HIGHEST
        )
        active = (block_rows[:, None] >= block_cols[None, :]) & (block_cols[None, :] > step)
        tiles = tiles - jnp.where(active[:, None, :, None], product, 0.0)
    return tiles.reshape(row_tiles, 1, tile, col_tiles, 1, tile)


def solution(mesh):
    return jax.shard_map(
        shards,
        mesh=mesh,
        in_specs=(P(None, None, ("row", "col")), P(None, ("row", "col")), P(("row", "col")), P()),
        out_specs=P(None, "row", None, None, "col", None),
        check_vma=False,
    )
```

profile of v0, /device:TPU:15, one launch (start us, length us, event | category | flops | bytes accessed | tf_op | source)
XLA Modules:
  0.0 1389.2 jit_solution(5200536761877793018)
XLA Ops:
  7.3 58.6 %all_gather.9 = f32[3,4,8192]{2,1,0:T(4,128)S(1)} all-gather(f32[3,4,256]{2,1,0:T(4,128)} %param.29), channel_id=1, replica_groups=mesh['row'=4,'col'=8] {'row','col'}, dimensions={2}, use_global_device_ids=true | all-gather | bytes 405504 | tf_op jit(solution)/shard_map/all_gather | solution.py:50
  65.9 66.1 %all_gather.10 = f32[4,8192]{1,0:T(4,128)S(1)} all-gather(f32[4,256]{1,0:T(4,128)} %param.30), channel_id=1, replica_groups=mesh['row'=4,'col'=8] {'row','col'}, dimensions={1}, use_global_device_ids=true | all-gather | bytes 135168 | tf_op jit(solution)/shard_map/all_gather | solution.py:51
  133.2 64.3 %all-gather = f32[32,1,256]{2,1,0:T(1,128)S(1)} all-gather(f32[1,1,256]{2,1,0:T(1,128)} %bitcast.705), channel_id=1, replica_groups=mesh['row'=4,'col'=8] {'row','col'}, dimensions={0}, use_global_device_ids=true | all-gather | bytes 33792 | tf_op jit(solution)/shard_map/all_gather | solution.py:52
  199.6 10.6 conditional.10
  199.9 8.8 select_add_fusion.2
  211.2 12.0 conditional.8
  212.7 8.8 select_add_fusion
  229.1 11.9 conditional.15
  230.7 8.8 select_add_fusion.7
  241.0 13.6 conditional.13
  242.9 8.8 select_add_fusion.5
  254.6 12.8 conditional.12
  256.1 8.8 select_add_fusion.4
  267.4 12.6 conditional.14
  268.6 8.8 select_add_fusion.6
  292.6 11.7 cholesky.286
  304.5 9.8 custom-call.27
  315.0 11.7 cholesky.305
  328.1 10.2 custom-call.28
  339.0 11.7 cholesky.326
  351.4 9.8 custom-call.29
  361.8 11.9 cholesky.343
  380.2 13.3 while.6
  394.6 158.0 %custom-call.30 = f32[4,4,128,128]{2,3,1,0:T(8,128)S(1)} custom-call(f32[4,4,128,128]{3,2,1,0:T(8,128)} %bitcast.443), custom_call_target="InvertDiagBlocksLowerTriangular" | custom-call | tf_op jit(solution)/shard_map/triangular_solve/custom-call.3 | solution.py:95
  562.4 3.6 fusion.33
  567.1 4.0 broadcast_select_fusion.2
  571.3 161.8 %all-reduce.10.cloned.1.call-done = f32[4,512,512]{1,2,0:T(8,128)} async-done(((f32[4,512,512]{1,2,0:T(8,128)}), f32[4,512,512]{1,2,0:T(8,128)}) %all-reduce.10.cloned.1.call-update) | async-done | bytes 4194320 | tf_op jit(solution)/shard_map/psum | solution.py:11
  737.8 5.3 bitcast_dynamic-update-slice_fusion.2
  743.2 46.2 %all-reduce.12.cloned.1.call-done = f32[2,512,512]{1,2,0:T(8,128)} async-done(((f32[2,512,512]{1,2,0:T(8,128)}), f32[2,512,512]{1,2,0:T(8,128)}) %all-reduce.12.cloned.1.call-update) | async-done | bytes 2097168 | tf_op jit(solution)/shard_map/psum | solution.py:11
  789.4 18.8 %select_subtract_fusion = f32[4,512,2,512]{1,3,2,0:T(8,128)S(1)} fusion(f32[4,512,2,512]{1,3,2,0:T(8,128)} %bitcast_dynamic-update-slice_fusion.2, pred[4,2]{1,0:T(4,128)(4,1)S(1)} %get-tuple-element.549, f32[4,512,512]{1,2,0:T(8,128)} %all-reduce.10.cloned.1.call-done, f32[2,512,512]{1,2,0:T(8,128)} %all-reduce.12.cloned.1.call-done), kind=kOutput, calls=%fused_computation.148 | convolution fusion | flops 12889096192 | bytes 23068680 | tf_op jit(solution)/shard_map/iab,jcb->iajc/dot_general | solution.py:108
  812.8 4.6 slice_bitcast_fusion
  817.4 31.7 %all-reduce.14.cloned.1.call-done = f32[512,512]{0,1:T(8,128)} async-done(((f32[512,512]{0,1:T(8,128)}), f32[512,512]{0,1:T(8,128)}) %all-reduce.14.cloned.1.call-update) | async-done | bytes 1048592 | tf_op jit(solution)/shard_map/psum | solution.py:11
  852.1 11.7 cholesky.358
  864.0 9.8 custom-call.31
  874.5 11.7 cholesky.377
  887.6 10.0 custom-call.32
  898.2 11.7 cholesky.398
  910.7 9.8 custom-call.33
  921.1 11.9 cholesky.415
  939.5 13.1 while.7
  953.7 158.0 %custom-call.34 = f32[4,4,128,128]{2,3,1,0:T(8,128)S(1)} custom-call(f32[4,4,128,128]{3,2,1,0:T(8,128)} %bitcast.442), custom_call_target="InvertDiagBlocksLowerTriangular" | custom-call | tf_op jit(solution)/shard_map/triangular_solve/custom-call.3 | solution.py:95
  1121.5 3.6 fusion.30
  1126.2 4.3 broadcast_select_fusion.1
  1130.6 155.5 %all-reduce.16.cloned.1.call-done = f32[4,512,512]{1,2,0:T(8,128)} async-done(((f32[4,512,512]{1,2,0:T(8,128)}), f32[4,512,512]{1,2,0:T(8,128)}) %all-reduce.16.cloned.1.call-update) | async-done | bytes 4194320 | tf_op jit(solution)/shard_map/psum | solution.py:11
  1290.7 5.4 bitcast_dynamic-update-slice_fusion.3
  1296.1 46.4 %all-reduce.18.cloned.1.call-done = f32[2,512,512]{1,2,0:T(8,128)} async-done(((f32[2,512,512]{1,2,0:T(8,128)}), f32[2,512,512]{1,2,0:T(8,128)}) %all-reduce.18.cloned.1.call-update) | async-done | bytes 2097168 | tf_op jit(solution)/shard_map/psum | solution.py:11
  1342.4 19.0 %subtract_bitcast_fusion = f32[4,1,512,2,1,512]{2,5,3,0,4,1:T(8,128)} fusion(f32[4,512,2,512]{1,3,2,0:T(8,128)} %bitcast_dynamic-update-slice_fusion.3, pred[4,2]{1,0:T(4,128)(4,1)S(1)} %get-tuple-element.548, f32[4,512,512]{1,2,0:T(8,128)} %all-reduce.16.cloned.1.call-done, f32[2,512,512]{1,2,0:T(8,128)} %all-reduce.18.cloned.1.call-done), kind=kOutput, calls=%fused_computation.147 | convolution fusion | flops 12889096192 | bytes 23068680 | tf_op jit(solution)/shard_map/iab,jcb->iajc/dot_general | solution.py:108
  1361.4 20.5 %copy.332 = f32[4,1,512,2,1,512]{5,4,3,2,1,0:T(1,128)} copy(f32[4,1,512,2,1,512]{2,5,3,0,4,1:T(8,128)} %subtract_bitcast_fusion) | data formatting | bytes 16777216 | tf_op jit(solution)/shard_map/reshape | solution.py:113
  (210 shorter events, 126.7 us)
Async XLA Ops:
  6.5 283.1 %all-reduce.8.cloned.1.call-start = ((), (), s32[]{:S(2)}) async-start(), calls=%async_computation | async-start | bytes 2097152 | tf_op jit(solution)/shard_map/psum | solution.py:11
  198.3 0.8 copy-start.8
  198.6 1.0 copy-start.5
  210.2 1.0 copy-start.6
  223.2 1.0 copy-start.7
  228.9 504.2 %all-reduce.10.cloned.1.call-start = ((), (), s32[]{:S(2)}) async-start(), calls=%async_computation.1 | async-start | bytes 8388608 | tf_op jit(solution)/shard_map/psum | solution.py:11
  280.0 2.7 copy-start.4
  283.8 3.4 copy-start.1
  393.5 1.1 copy-start.10
  552.6 5.9 copy-start.2
  558.6 8.5 slice-start.2
  562.4 4.7 slice-start.3
  571.1 218.2 %all-reduce.12.cloned.1.call-start = ((), (), s32[]{:S(2)}) async-start(), calls=%async_computation.2 | async-start | bytes 4194304 | tf_op jit(solution)/shard_map/psum | solution.py:11
  737.7 111.4 %all-reduce.14.cloned.1.call-start = ((), (), s32[]{:S(2)}) async-start(), calls=%async_computation.3 | async-start | bytes 2097152 | tf_op jit(solution)/shard_map/psum | solution.py:11
  808.2 3.4 copy-start
  812.7 473.4 %all-reduce.16.cloned.1.call-start = ((), (), s32[]{:S(2)}) async-start(), calls=%async_computation.4 | async-start | bytes 8388608 | tf_op jit(solution)/shard_map/psum | solution.py:11
  952.6 1.1 copy-start.9
  1111.7 5.9 copy-start.3
  1117.7 8.5 slice-start
  1121.5 4.7 slice-start.1
  1130.5 211.9 %all-reduce.18.cloned.1.call-start = ((), (), s32[]{:S(2)}) async-start(), calls=%async_computation.5 | async-start | bytes 4194304 | tf_op jit(solution)/shard_map/psum | solution.py:11
Sparse Core Ops, SparseCore 0:
  229.0 43.1 all-reduce.7
  571.3 161.7 all-reduce.9
  737.8 51.5 all-reduce.11
  812.9 36.1 all-reduce.13
  1130.7 155.3 all-reduce.15
  1290.8 51.5 all-reduce.17
where the time goes:
time: 1400 us; the launch traced here: 1390 us
  other arithmetic  570 us (41%)
  waiting for transfers between devices  442 us (32%)
  blocking collectives  189 us (14%)
  local copies, waits for them, and re-layouts  97.4 us (7%)
  matrix products  70.3 us (5%)
  between operations  20.1 us (1%)
    psum x6, waiting for transfers between devices, broadcast(): return lax.psum(kept, axis)  442 us
    another operation x6, other arithmetic, shards(): lax.linalg.triangular_solve(repeated, column, left_side=False, lower=True...  321 us
    another operation x30, other arithmetic, shards(): diagonal_factor = jnp.linalg.cholesky(diagonal)  159 us
    all_gather x1, blocking collectives, shards(): lax.all_gather(weights, ('row', 'col'), axis=1, tiled=True)  66.1 us
    all_gather x1, blocking collectives, shards(): lax.all_gather(shift, ('row', 'col'), axis=0, tiled=True)  64.3 us
    all_gather x1, blocking collectives, shards(): lax.all_gather(points, ('row', 'col'), axis=2, tiled=True)  58.6 us
    add x6, other arithmetic, assemble(): values + jnp.where(row_ids[:, None] == col_ids[None, :], row_shift[:, Non...  52.6 us
    dot_general x2, matrix products, shards(): jnp.einsum('iab,jcb->iajc', row_factors, col_factors, precision=lax.Preci...  37.8 us
  transfers between devices with their start and end apart: 6, of which 5 were waited for; matrix products, arithmetic and copies ran while one was open for 5% of the time, Pallas kernels for 0%

commit v1 on v0

v1 whole, which is shorter than its diff:
```python
import functools

import jax
import jax.numpy as jnp
from jax import lax
from jax.experimental import pallas as pl
from jax.experimental.pallas import tpu as pltpu
from jax.sharding import PartitionSpec as P

SOFTENING_SQUARED = 0.0004
HIGHEST = lax.Precision.HIGHEST
FEATURES = 48
BLOCK = 128
ROWS = 64


def gather_kernel(row_count, col_count, own, out, local_sem, send_col, recv_col, send_row, recv_row):
    row = lax.axis_index("row")
    col = lax.axis_index("col")
    barrier = pltpu.get_barrier_semaphore()
    for step in range(1, col_count):
        peer = lax.rem(col + step, col_count)
        pl.semaphore_signal(barrier, inc=1, device_id={"col": peer}, device_id_type=pl.DeviceIdType.MESH)
    for step in range(1, row_count):
        peer = lax.rem(row + step, row_count)
        pl.semaphore_signal(barrier, inc=1, device_id={"row": peer}, device_id_type=pl.DeviceIdType.MESH)
    pl.semaphore_wait(barrier, row_count + col_count - 2)
    keep = pltpu.make_async_copy(own, out.at[row, col], local_sem)
    keep.start()
    copies = []
    for step in range(1, col_count):
        peer = lax.rem(col + step, col_count)
        copies.append(
            pltpu.make_async_remote_copy(
                src_ref=own,
                dst_ref=out.at[row, col],
                send_sem=send_col.at[step - 1],
                recv_sem=recv_col.at[step - 1],
                device_id={"col": peer},
                device_id_type=pl.DeviceIdType.MESH,
            )
        )
        copies[-1].start()
    keep.wait()
    for copy in copies:
        copy.wait()
    copies = []
    for step in range(1, row_count):
        peer = lax.rem(row + step, row_count)
        copies.append(
            pltpu.make_async_remote_copy(
                src_ref=out.at[row],
                dst_ref=out.at[row],
                send_sem=send_row.at[step - 1],
                recv_sem=recv_row.at[step - 1],
                device_id={"row": peer},
                device_id_type=pl.DeviceIdType.MESH,
            )
        )
        copies[-1].start()
    for copy in copies:
        copy.wait()


def gather(own, row_count, col_count):
    return pl.pallas_call(
        functools.partial(gather_kernel, row_count, col_count),
        out_shape=jax.ShapeDtypeStruct((row_count, col_count) + own.shape, own.dtype),
        in_specs=[pl.BlockSpec(memory_space=pltpu.VMEM)],
        out_specs=pl.BlockSpec(memory_space=pltpu.VMEM),
        scratch_shapes=[
            pltpu.SemaphoreType.DMA,
            pltpu.SemaphoreType.DMA((col_count - 1,)),
            pltpu.SemaphoreType.DMA((col_count - 1,)),
            pltpu.SemaphoreType.DMA((row_count - 1,)),
            pltpu.SemaphoreType.DMA((row_count - 1,)),
        ],
        compiler_params=pltpu.CompilerParams(collective_id=0, has_side_effects=True),
        name="gather_panels",
    )(own)


def dot(left, right, precision=None):
    return lax.dot_general(
        left, right, (((1,), (0,)), ((), ())), precision=precision, preferred_element_type=jnp.float32
    )


def dot_transposed(left, right, precision=None):
    return lax.dot_general(
        left, right, (((1,), (1,)), ((), ())), precision=precision, preferred_element_type=jnp.float32
    )


def split(value):
    high = value.astype(jnp.bfloat16)
    return high, (value - high.astype(jnp.float32)).astype(jnp.bfloat16)


def factor_block(source, upper, inverse, side):
    row_ids = lax.broadcasted_iota(jnp.int32, (BLOCK, BLOCK), 0)
    col_ids = lax.broadcasted_iota(jnp.int32, (BLOCK, BLOCK), 1)
    eight = lax.broadcasted_iota(jnp.int32, (8, BLOCK), 0)
    empty = jnp.zeros((8, BLOCK), jnp.float32)

    def panel(index, state):
        values, companion = state
        side(index)
        upper_rows, inverse_rows = empty, empty
        for j in range(8):
            scale = lax.rsqrt(values[j : j + 1, j : j + 1])
            pivot_row = values[j : j + 1, :] * scale
            companion_row = companion[j : j + 1, :] * scale
            column = jnp.broadcast_to(values[:, j : j + 1], (BLOCK, BLOCK)) * scale
            column = jnp.where(row_ids > j, column, 0.0)
            upper_rows = jnp.where(eight == j, pivot_row, upper_rows)
            inverse_rows = jnp.where(eight == j, companion_row, inverse_rows)
            values = values - column * pivot_row
            companion = companion - column * companion_row
        start = pl.multiple_of(index * 8, 8)
        upper[pl.ds(start, 8), :] = pltpu.roll(upper_rows, start, 1)
        inverse[pl.ds(start, 8), :] = inverse_rows
        values = pltpu.roll(jnp.concatenate([values[8:], empty], axis=0), BLOCK - 8, 1)
        companion = jnp.concatenate([companion[8:], empty], axis=0)
        return values, companion

    identity = jnp.where(row_ids == col_ids, 1.0, 0.0)
    lax.fori_loop(0, BLOCK // 8, panel, (source, identity))
    return jnp.where(col_ids >= row_ids, upper[...], 0.0).T, inverse[...]


def factor_tile(matrix, lower, inverse, upper_block, inverse_block, side):
    tile = matrix.shape[0]
    count = tile // BLOCK
    lower[...] = jnp.zeros((tile, tile), jnp.float32)
    inverse[...] = jnp.zeros((tile, tile), jnp.float32)
    for k in range(count):
        here = slice(k * BLOCK, (k + 1) * BLOCK)
        below = slice((k + 1) * BLOCK, tile)
        first = k * (BLOCK // 8)
        diagonal, block = factor_block(
            matrix[here, here], upper_block, inverse_block, lambda index: side(first + index)
        )
        lower[here, here] = diagonal
        inverse[here, here] = block
        if k + 1 < count:
            solved = dot_transposed(matrix[below, here], block, HIGHEST)
            lower[below, here] = solved
            matrix[below, below] = matrix[below, below] - dot_transposed(solved, solved, HIGHEST)
    size = BLOCK
    while size < tile:
        for start in range(0, tile, 2 * size):
            top = slice(start, start + size)
            bottom = slice(start + size, start + 2 * size)
            inner = dot(lower[bottom, top], inverse[top, top], HIGHEST)
            inverse[bottom, top] = -dot(inverse[bottom, bottom], inner, HIGHEST)
        size *= 2


def main_kernel(
    row_tiles, col_tiles, own_count,
    plan, own_plan, left, right, exact,
    out,
    tiles, matrix, lower0, lower1, inverse, inverse_high, inverse_low, first_high, first_low,
    panel_high, panel_low, upper_block, inverse_block,
):
    tile = matrix.shape[0]
    quadrature = right.shape[1]
    chunks = tile // ROWS
    listed = 2 + row_tiles + col_tiles
    work = plan.shape[0] // 4

    def assemble(item, chunk):
        left_index, right_index = plan[4 * item], plan[4 * item + 1]
        diagonal = plan[4 * item + 2]
        start = pl.multiple_of(chunk * ROWS, ROWS)
        row_ids = lax.broadcasted_iota(jnp.int32, (ROWS, tile), 0) + start
        col_ids = lax.broadcasted_iota(jnp.int32, (ROWS, tile), 1)
        on_diagonal = (row_ids - col_ids) == jnp.where(diagonal == 1, 0, 2 * tile)
        features = left[left_index, chunk]
        total = jnp.zeros((ROWS, tile), jnp.float32)
        for second in range(quadrature):
            squared = dot(features, right[right_index, second])
            for first in range(quadrature):
                part = squared[first * ROWS : (first + 1) * ROWS]
                if first == second:
                    part = jnp.where(on_diagonal, exact[right_index, second : second + 1, :], part)
                total = total + lax.rsqrt(part)
        shifted = exact[right_index, quadrature : quadrature + 1, :]
        tiles[item, pl.ds(start, ROWS), :] = total + jnp.where(on_diagonal, shifted, 0.0)

    def assemble_tile(item):
        def step(chunk, carry):
            assemble(item, chunk)
            return carry
        lax.fori_loop(0, chunks, step, 0)

    def side_from(first_item):
        def side(index):
            assemble(first_item + index // chunks, lax.rem(index, chunks))
        return side

    panels = tile // 8
    covered = panels // chunks
    assemble_tile(0)
    matrix[...] = tiles[0]
    factor_tile(matrix, lower0, inverse, upper_block, inverse_block, side_from(1))
    inverse_high[0], inverse_low[0] = split(inverse[...].T)

    def three(left_high, left_low, right_high, right_low, multiply):
        return (
            multiply(left_high, right_high)
            + multiply(left_high, right_low)
            + multiply(left_low, right_high)
        )

    def solve_first(index, carry):
        high, low = split(tiles[index])
        solved = three(high, low, inverse_high[0], inverse_low[0], dot)
        high, low = split(solved)
        panel_high[index - 1, :, :tile] = high
        panel_low[index - 1, :, :tile] = low
        return carry

    lax.fori_loop(1, listed, solve_first, 0)
    first_high[...] = panel_high[0, :, :tile]
    first_low[...] = panel_low[0, :, :tile]

    def reduce_second(index, carry):
        update = three(
            panel_high[index - 1, :, :tile], panel_low[index - 1, :, :tile],
            first_high[...], first_low[...], dot_transposed,
        )
        item = listed - 1 + index
        tiles[item] = tiles[item] - update
        return carry

    reduce_second(1, 0)
    matrix[...] = tiles[listed]
    factor_tile(matrix, lower1, inverse, upper_block, inverse_block, side_from(1 + covered))
    inverse_high[1], inverse_low[1] = split(inverse[...].T)
    done = 1 + 2 * covered

    def solve_second(index, carry):
        reduce_second(index, carry)
        high, low = split(tiles[listed - 1 + index])
        solved = three(high, low, inverse_high[1], inverse_low[1], dot)
        high, low = split(solved)
        panel_high[index - 1, :, tile:] = high
        panel_low[index - 1, :, tile:] = low
        return carry

    lax.fori_loop(2, listed, solve_second, 0)

    def rest(item, carry):
        @pl.when(plan[4 * item + 3] == 1)
        def _():
            assemble_tile(item)
        return carry

    lax.fori_loop(done, work, rest, 0)

    lanes = tile // BLOCK
    pitch = col_tiles * lanes

    def store(i, j, value):
        for q in range(lanes):
            out[pl.ds(i * tile * pitch + j * lanes + q, tile, stride=pitch), :] = value[
                :, q * BLOCK : (q + 1) * BLOCK
            ]

    def finish(index, carry):
        i, j = index // col_tiles, lax.rem(index, col_tiles)
        kind = own_plan[2 * index]

        @pl.when(kind == 0)
        def _():
            store(i, j, jnp.zeros((tile, tile), jnp.float32))

        @pl.when(kind == 1)
        def _():
            store(i, j, lower0[...])

        @pl.when(kind == 2)
        def _():
            value = panel_high[1 + i, :, :tile].astype(jnp.float32)
            store(i, j, value + panel_low[1 + i, :, :tile].astype(jnp.float32))

        @pl.when(kind == 3)
        def _():
            store(i, j, lower1[...])

        @pl.when(kind == 4)
        def _():
            value = panel_high[1 + i, :, tile:].astype(jnp.float32)
            store(i, j, value + panel_low[1 + i, :, tile:].astype(jnp.float32))

        @pl.when(kind == 5)
        def _():
            update = three(
                panel_high[1 + i], panel_low[1 + i],
                panel_high[1 + row_tiles + j], panel_low[1 + row_tiles + j], dot_transposed,
            )
            store(i, j, tiles[own_plan[2 * index + 1]] - update)

        return carry

    lax.fori_loop(0, row_tiles * col_tiles, finish, 0)


def pieces(value):
    parts = []
    for _ in range(3):
        part = lax.reduce_precision(value, 8, 7)
        parts.append(part)
        value = value - part
    return parts


def shards(points, weights, shift, cluster_rank):
    row_count = lax.axis_size("row")
    col_count = lax.axis_size("col")
    row_index = lax.axis_index("row")
    col_index = lax.axis_index("col")
    quadrature, length = weights.shape
    clusters = cluster_rank.shape[0]
    tile = length * row_count * col_count // clusters
    row_tiles = clusters // row_count
    col_tiles = clusters // col_count

    own = jnp.concatenate([points.reshape(3 * quadrature, length), weights, shift[None]], axis=0)
    rows = own.shape[0]
    own = jnp.pad(own, ((0, -rows % 8), (0, 0)))
    everything = gather(own, row_count, col_count)

    block_rows = jnp.arange(row_tiles, dtype=jnp.int32) * row_count + row_index
    block_cols = jnp.arange(col_tiles, dtype=jnp.int32) * col_count + col_index
    places = jnp.concatenate([jnp.arange(2, dtype=jnp.int32), block_rows, block_cols])
    listed = places.shape[0]
    names = jnp.arange(clusters, dtype=jnp.int32)
    chosen = jnp.sum(
        jnp.where(cluster_rank[None, :] == places[:, None], names[None, :], 0), axis=1
    )
    everything = everything.reshape(clusters, tile // length, -1, length)
    local = jnp.take(everything, chosen, axis=0)[:, :, :rows]
    local = jnp.transpose(local, (2, 0, 1, 3)).reshape(rows, listed, tile)
    coordinates = local[: 3 * quadrature].reshape(3, quadrature, listed, tile) - 0.5
    weight = local[3 * quadrature : 4 * quadrature]
    shifted = local[4 * quadrature]
    scale = 1.0 / (weight * weight)
    norm = jnp.sum(coordinates * coordinates, axis=0)
    left_parts = pieces(
        jnp.concatenate(
            [-2.0 * coordinates * scale, ((norm + SOFTENING_SQUARED) * scale)[None], scale[None]]
        )
    )
    right_parts = pieces(
        jnp.concatenate([coordinates * scale, scale[None], (norm * scale)[None]])
    )
    left = jnp.concatenate([left_parts[i] for i in range(3) for _ in range(3)])
    right = jnp.concatenate([right_parts[i] for _ in range(3) for i in range(3)])
    padding = ((0, FEATURES - left.shape[0]), (0, 0), (0, 0), (0, 0))
    left = jnp.pad(left.astype(jnp.bfloat16), padding)
    right = jnp.pad(right.astype(jnp.bfloat16), padding)
    left = left.reshape(FEATURES, quadrature, listed, tile // ROWS, ROWS)
    left = jnp.transpose(left, (2, 3, 1, 4, 0)).reshape(
        listed, tile // ROWS, quadrature * ROWS, FEATURES
    )
    right = jnp.transpose(right, (2, 1, 0, 3))
    exact = jnp.concatenate([SOFTENING_SQUARED * scale * scale, shifted[None]])
    exact = jnp.pad(jnp.transpose(exact, (1, 0, 2)), ((0, 0), (0, -exact.shape[0] % 8), (0, 0)))

    own_rows = jnp.repeat(jnp.arange(row_tiles, dtype=jnp.int32), col_tiles)
    own_cols = jnp.tile(jnp.arange(col_tiles, dtype=jnp.int32), row_tiles)
    tile_row, tile_col = block_rows[own_rows], block_cols[own_cols]
    active = (tile_row >= tile_col) & (tile_col >= 2)
    own_count = max(
        sum(
            i * row_count + r >= j * col_count + c
            for i in range(row_tiles)
            for j in range(col_tiles)
        )
        for r in range(row_count)
        for c in range(col_count)
    )
    slot = jnp.cumsum(active.astype(jnp.int32)) - 1
    takes = active[None, :] & (slot[None, :] == jnp.arange(own_count, dtype=jnp.int32)[:, None])

    def placed(values):
        return jnp.sum(jnp.where(takes, values[None, :], 0), axis=1)

    ordered = jnp.arange(1, listed, dtype=jnp.int32)
    zero = jnp.zeros((1,), jnp.int32)
    left_index = jnp.concatenate([zero, ordered, ordered, placed(own_rows + 2)])
    right_index = jnp.concatenate(
        [zero, 0 * ordered, 0 * ordered + 1, placed(own_cols + 2 + row_tiles)]
    )
    used = jnp.concatenate(
        [zero + 1, 0 * ordered + 1, 0 * ordered + 1, placed(active.astype(jnp.int32))]
    )
    diagonal = (places[left_index] == places[right_index]).astype(jnp.int32)
    plan = jnp.stack([left_index, right_index, diagonal, used], axis=1).reshape(-1)
    kind = jnp.where(
        tile_row < tile_col, 0,
        jnp.where(
            tile_col >= 2, 5,
            jnp.where(tile_col == 0, jnp.where(tile_row == 0, 1, 2), jnp.where(tile_row == 1, 3, 4)),
        ),
    ).astype(jnp.int32)
    base = 2 * listed - 1
    own_plan = jnp.stack([kind, base + jnp.where(active, slot, 0)], axis=1).reshape(-1).astype(jnp.int32)

    work = base + own_count
    whole = pl.BlockSpec(memory_space=pltpu.VMEM)
    scalars = pl.BlockSpec(memory_space=pltpu.SMEM)
    f32, bf16 = jnp.float32, jnp.bfloat16
    result = pl.pallas_call(
        functools.partial(main_kernel, row_tiles, col_tiles, own_count),
        out_shape=jax.ShapeDtypeStruct((row_tiles * tile * col_tiles * tile // BLOCK, BLOCK), f32),
        in_specs=[scalars, scalars, whole, whole, whole],
        out_specs=whole,
        scratch_shapes=[
            pltpu.VMEM((work, tile, tile), f32),
            pltpu.VMEM((tile, tile), f32),
            pltpu.VMEM((tile, tile), f32),
            pltpu.VMEM((tile, tile), f32),
            pltpu.VMEM((tile, tile), f32),
            pltpu.VMEM((2, tile, tile), bf16),
            pltpu.VMEM((2, tile, tile), bf16),
            pltpu.VMEM((tile, tile), bf16),
            pltpu.VMEM((tile, tile), bf16),
            pltpu.VMEM((listed - 1, tile, 2 * tile), bf16),
            pltpu.VMEM((listed - 1, tile, 2 * tile), bf16),
            pltpu.VMEM((BLOCK, BLOCK), f32),
            pltpu.VMEM((BLOCK, BLOCK), f32),
        ],
        compiler_params=pltpu.CompilerParams(vmem_limit_bytes=63 * 1024 * 1024),
        name="assemble_and_factor",
    )(plan, own_plan, left, right, exact)
    return result.reshape(row_tiles, 1, tile, col_tiles, 1, tile)


def solution(mesh):
    return jax.shard_map(
        shards,
        mesh=mesh,
        in_specs=(P(None, None, ("row", "col")), P(None, ("row", "col")), P(("row", "col")), P()),
        out_specs=P(None, "row", None, None, "col", None),
        check_vma=False,
    )
```

time: 1400 us -> 255 us (0.18)
  other arithmetic: 570 us -> 3.51 us
  waiting for transfers between devices: 442 us -> 0 us
  Pallas kernels: 0 us -> 228 us
  blocking collectives: 189 us -> 0 us
  local copies, waits for them, and re-layouts: 97.4 us -> 22.6 us
  matrix products: 70.3 us -> 0 us
  between operations: 20.1 us -> 0.37 us
    another operation x39 -> x6, other arithmetic: 488 us -> 0.62 us  [the longest x6 321 us: shards(): lax.linalg.triangular_solve(repeated, column, left_side=False, lower=True...]
    psum x6 -> x0, waiting for transfers between devices: 442 us -> none  [broadcast(): return lax.psum(kept, axis)]
    pallas_call x0 -> x2, Pallas kernels: none -> 228 us  [the longest x1 209 us: shards(): pl.pallas_call(functools.partial(main_kernel, row_tiles, col_tiles, own_c...]
    all_gather x3 -> x0, blocking collectives: 189 us -> none  [the longest x1 66.1 us: shards(): lax.all_gather(weights, ('row', 'col'), axis=1, tiled=True)]
    add x12 -> x4, other arithmetic: 52.6 us -> 0.02 us  [the longest x1 0.01 us: shards(): base + jnp.where(active, slot, 0)]
    dot_general x2 -> x0, matrix products: 37.8 us -> none  [shards(): jnp.einsum('iab,jcb->iajc', row_factors, col_factors, precision=lax.Preci...]
    another operation x26 -> x0, matrix products: 32.5 us -> none  [the longest x14 28.8 us: shards(): lax.linalg.triangular_solve(repeated, column, left_side=False, lower=True...]
    another operation x53 -> x7, local copies, waits for them, and re-layouts: 26.8 us -> 0.27 us  [the longest x1 0.1 us: shards(): jnp.stack([left_index, right_index, diagonal, used], axis=1).reshape(-1)]
  transfers between devices with their start and end apart: 6 -> 0, of which waited for: 5 -> 0; matrix products, arithmetic and copies ran while one was open for 5% -> 0% of each run, Pallas kernels for 0% -> 0%
where the time goes in v1:
time: 255 us; the launch traced here: 254 us
  Pallas kernels  228 us (89%)
  local copies, waits for them, and re-layouts  22.6 us (9%)
  other arithmetic  3.51 us (1%)
    pallas_call x1, Pallas kernels, shards(): pl.pallas_call(functools.partial(main_kernel, row_tiles, col_tiles, own_c...  209 us
    pallas_call x1, Pallas kernels, gather(): pl.pallas_call(functools.partial(gather_kernel, row_count, col_count), ou...  19.4 us
    reshape x2, local copies, waits for them, and re-layouts, shards(): left = left.reshape(FEATURES, quadrature, listed, tile // ROWS, ROWS)  9.14 us

profile of v1, /device:TPU:15, one launch (start us, length us, event | category | flops | bytes accessed | tf_op | source)
XLA Modules:
  0.0 254.4 jit_solution(11028455337167065916)
XLA Ops:
  0.0 0.0 copy-start.2
  0.0 0.0 copy-start.1
  0.0 0.0 copy-start
  0.1 0.1 pad_add_fusion.7
  0.1 0.8 select_reduce_fusion
  1.0 0.1 add.173
  1.1 0.1 add.176
  1.2 0.1 tile.12
  1.3 0.1 reshape.527
  1.4 0.6 gather_fusion
  2.0 0.6 gather_fusion.1
  2.7 0.2 reduce-window.4
  2.9 0.1 select_reduce_fusion.2
  3.1 0.1 fusion.19
  3.1 0.1 fusion.22
  3.3 0.1 fusion.10
  3.4 0.1 fusion.20
  3.4 0.1 copy.44
  3.5 0.6 reshape.529.own_plan
  4.1 0.7 gather_fusion.2
  4.8 0.7 gather_fusion.3
  5.6 0.1 copy.43
  5.7 0.7 reshape.528.plan
  6.3 0.0 copy-done
  6.4 0.0 copy-done.2
  6.4 0.0 copy-done.1
  6.4 0.6 select_maximum_fusion.own
  7.0 19.4 %gather_panels.1 = f32[4,8,24,256]{3,2,1,0:T(8,128)} custom-call(f32[24,256]{1,0:T(8,128)} %select_maximum_fusion.own), custom_call_target="tpu_custom_call" | custom-call | tf_op jit(solution)/shard_map/gather_panels/pallas_call | solution.py:66
  26.4 1.7 gather_fusion.4
  28.1 0.2 fusion.4
  28.5 0.1 div.31
  28.6 0.1 div.30
  28.7 0.7 pad.18.exact
  29.4 0.2 copy_multiply_fusion
  29.6 0.1 copy_multiply_fusion.1
  29.8 0.3 fusion.1
  30.1 3.6 %concatenate.101 = bf16[45,4,8,512]{3,0,1,2:T(8,128)(2,1)S(1)} concatenate(bf16[5,4,8,512]{3,0,1,2:T(8,128)(2,1)S(1)} %get-tuple-element.12, bf16[5,4,8,512]{3,0,1,2:T(8,128)(2,1)S(1)} %get-tuple-element.11, bf16[5,4,8,512]{3,0,1,2:T(8,128)(2,1)S(1)} %get-tuple-element.10, bf16[5,4,8,512]{3,0,1,2:T(8,128)(2,1)S(1)} %get-tuple-element.12, ...), dimensions={0} | concatenate | bytes 2949120 | tf_op jit(solution)/shard_map/concatenate | solution.py:361
  33.7 1.4 pad_bitcast_fusion.right
  35.3 0.1 constant_dynamic-update-slice_fusion.2
  35.3 0.1 constant_dynamic-update-slice_fusion.1
  35.4 0.1 constant_dynamic-update-slice_fusion
  35.4 1.3 pad.16
  36.7 3.9 %reshape.532 = bf16[48,4,8,8,64]{4,3,2,1,0:T(8,128)(2,1)S(1)} reshape(bf16[48,4,8,512]{3,2,1,0:T(8,128)(2,1)} %pad.16) | data formatting | bytes 3145728 | tf_op jit(solution)/shard_map/reshape | solution.py:365
  40.7 5.2 %copy.52 = bf16[48,4,8,8,64]{0,4,1,3,2:T(8,128)(2,1)} copy(bf16[48,4,8,8,64]{4,3,2,1,0:T(8,128)(2,1)S(1)} %reshape.532) | data formatting | bytes 3145728 | tf_op jit(solution)/shard_map/reshape | solution.py:365
  45.9 208.5 %assemble_and_factor.1 = f32[16384,128]{1,0:T(8,128)} custom-call(s32[84]{0:T(128)} %reshape.528.plan, s32[16]{0:T(128)} %reshape.529.own_plan, bf16[8,8,256,48]{3,2,1,0:T(8,128)(2,1)} %bitcast.75, bf16[8,4,48,512]{3,2,1,0:T(8,128)(2,1)} %pad_bitcast_fusion.right, f32[8,8,512]{2,1,0:T(8,128)} %pad.18.exact), custom_call_target="tpu_custom_call" | custom-call | tf_op jit(solution)/shard_map/assemble_and_factor/pallas_call | solution.py:417
  (45 shorter events, 0.6 us)
Async XLA Ops:
  0.0 6.4 %copy-start.2 = (f32[256]{0:T(256)S(1)}, f32[256]{0:T(256)}, u32[]{:S(2)}) copy-start(f32[256]{0:T(256)} %param.6) | copy-start | bytes 3076
  0.0 6.4 %copy-start.1 = (f32[4,256]{1,0:T(4,128)S(1)}, f32[4,256]{1,0:T(4,128)}, u32[]{:S(2)}) copy-start(f32[4,256]{1,0:T(4,128)} %param.5) | copy-start | bytes 12292
  0.0 6.3 %copy-start = (f32[3,4,256]{2,1,0:T(4,128)S(1)}, f32[3,4,256]{2,1,0:T(4,128)}, u32[]{:S(2)}) copy-start(f32[3,4,256]{2,1,0:T(4,128)} %param.4) | copy-start | bytes 36868

commit v2 on v1

--- a/solution.py
+++ b/solution.py
@@ -9,7 +9,7 @@
 
 SOFTENING_SQUARED = 0.0004
 HIGHEST = lax.Precision.HIGHEST
-FEATURES = 48
+FEATURES = 32
 BLOCK = 128
 ROWS = 64
 
@@ -108,11 +108,12 @@
         side(index)
         upper_rows, inverse_rows = empty, empty
         for j in range(8):
-            scale = lax.rsqrt(values[j : j + 1, j : j + 1])
+            column = jnp.broadcast_to(values[:, j : j + 1], values.shape)
+            scale = lax.rsqrt(column[j : j + 1, :])
             pivot_row = values[j : j + 1, :] * scale
             companion_row = companion[j : j + 1, :] * scale
-            column = jnp.broadcast_to(values[:, j : j + 1], (BLOCK, BLOCK)) * scale
-            column = jnp.where(row_ids > j, column, 0.0)
+            column = column * scale
+            column = jnp.concatenate([jnp.where(eight > j, column[:8], 0.0), column[8:]], axis=0)
             upper_rows = jnp.where(eight == j, pivot_row, upper_rows)
             inverse_rows = jnp.where(eight == j, companion_row, inverse_rows)
             values = values - column * pivot_row
@@ -125,7 +126,10 @@
         return values, companion
 
     identity = jnp.where(row_ids == col_ids, 1.0, 0.0)
-    lax.fori_loop(0, BLOCK // 8, panel, (source, identity))
+    middle = BLOCK // 16
+    values, companion = lax.fori_loop(0, middle, panel, (source, identity))
+    live = BLOCK // 2
+    lax.fori_loop(middle, 2 * middle, panel, (values[:live], companion[:live]))
     return jnp.where(col_ids >= row_ids, upper[...], 0.0).T, inverse[...]
 
 
@@ -174,20 +178,26 @@
         left_index, right_index = plan[4 * item], plan[4 * item + 1]
         diagonal = plan[4 * item + 2]
         start = pl.multiple_of(chunk * ROWS, ROWS)
-        row_ids = lax.broadcasted_iota(jnp.int32, (ROWS, tile), 0) + start
-        col_ids = lax.broadcasted_iota(jnp.int32, (ROWS, tile), 1)
-        on_diagonal = (row_ids - col_ids) == jnp.where(diagonal == 1, 0, 2 * tile)
+        wide = 2 * BLOCK
         features = left[left_index, chunk]
-        total = jnp.zeros((ROWS, tile), jnp.float32)
-        for second in range(quadrature):
-            squared = dot(features, right[right_index, second])
-            for first in range(quadrature):
-                part = squared[first * ROWS : (first + 1) * ROWS]
-                if first == second:
-                    part = jnp.where(on_diagonal, exact[right_index, second : second + 1, :], part)
-                total = total + lax.rsqrt(part)
-        shifted = exact[right_index, quadrature : quadrature + 1, :]
-        tiles[item, pl.ds(start, ROWS), :] = total + jnp.where(on_diagonal, shifted, 0.0)
+        offsets = lax.broadcasted_iota(jnp.int32, (ROWS, wide), 1) - lax.broadcasted_iota(
+            jnp.int32, (ROWS, wide), 0
+        )
+        origin = jnp.where(diagonal == 1, start, 2 * tile)
+        for half in range(0, tile, wide):
+            here = slice(half, half + wide)
+            on_diagonal = offsets == origin - half
+            total = jnp.zeros((ROWS, wide), jnp.float32)
+            for second in range(quadrature):
+                squared = dot(features, right[right_index, second, :, here])
+                for first in range(quadrature):
+                    part = squared[first * ROWS : (first + 1) * ROWS]
+                    if first == second:
+                        same = exact[right_index, second : second + 1, here]
+                        part = jnp.where(on_diagonal, same, part)
+                    total = total + lax.rsqrt(part)
+            shifted = exact[right_index, quadrature : quadrature + 1, here]
+            tiles[item, pl.ds(start, ROWS), here] = total + jnp.where(on_diagonal, shifted, 0.0)
 
     def assemble_tile(item):
         def step(chunk, carry):
@@ -214,12 +224,20 @@
             + multiply(left_low, right_high)
         )
 
+    def solve(value, step, target):
+        high, low = split(value)
+        half = tile // 2
+        for depth, first in ((half, 0), (tile, half)):
+            columns = slice(first, first + half)
+            solved = three(
+                high[:, :depth], low[:, :depth],
+                inverse_high[step, :depth, columns], inverse_low[step, :depth, columns], dot,
+            )
+            into = slice(step * tile + first, step * tile + first + half)
+            panel_high[target, :, into], panel_low[target, :, into] = split(solved)
+
     def solve_first(index, carry):
-        high, low = split(tiles[index])
-        solved = three(high, low, inverse_high[0], inverse_low[0], dot)
-        high, low = split(solved)
-        panel_high[index - 1, :, :tile] = high
-        panel_low[index - 1, :, :tile] = low
+        solve(tiles[index], 0, index - 1)
         return carry
 
     lax.fori_loop(1, listed, solve_first, 0)
@@ -243,11 +261,7 @@
 
     def solve_second(index, carry):
         reduce_second(index, carry)
-        high, low = split(tiles[listed - 1 + index])
-        solved = three(high, low, inverse_high[1], inverse_low[1], dot)
-        high, low = split(solved)
-        panel_high[index - 1, :, tile:] = high
-        panel_low[index - 1, :, tile:] = low
+        solve(tiles[listed - 1 + index], 1, index - 1)
         return carry
 
     lax.fori_loop(2, listed, solve_second, 0)
@@ -357,8 +371,9 @@
     right_parts = pieces(
         jnp.concatenate([coordinates * scale, scale[None], (norm * scale)[None]])
     )
-    left = jnp.concatenate([left_parts[i] for i in range(3) for _ in range(3)])
-    right = jnp.concatenate([right_parts[i] for _ in range(3) for i in range(3)])
+    pairs = [(0, 0), (0, 1), (1, 0), (1, 1), (0, 2), (2, 0)]
+    left = jnp.concatenate([left_parts[i] for i, _ in pairs])
+    right = jnp.concatenate([right_parts[i] for _, i in pairs])
     padding = ((0, FEATURES - left.shape[0]), (0, 0), (0, 0), (0, 0))
     left = jnp.pad(left.astype(jnp.bfloat16), padding)
     right = jnp.pad(right.astype(jnp.bfloat16), padding)

time: 255 us -> 208 us (0.82)
  Pallas kernels: 228 us -> 186 us
  local copies, waits for them, and re-layouts: 22.6 us -> 17.1 us
    pallas_call x1, Pallas kernels: 209 us -> 167 us  [shards(): pl.pallas_call(functools.partial(main_kernel, row_tiles, col_tiles, own_c...]
    reshape x2, local copies, waits for them, and re-layouts: 9.14 us -> 5.4 us  [shards(): left = left.reshape(FEATURES, quadrature, listed, tile // ROWS, ROWS)]
where the time goes in v2:
time: 208 us; the launch traced here: 207 us
  Pallas kernels  186 us (89%)
  local copies, waits for them, and re-layouts  17.1 us (8%)
  other arithmetic  4.06 us (2%)
    pallas_call x1, Pallas kernels, shards(): pl.pallas_call(functools.partial(main_kernel, row_tiles, col_tiles, own_c...  167 us
    pallas_call x1, Pallas kernels, gather(): pl.pallas_call(functools.partial(gather_kernel, row_count, col_count), ou...  19.4 us
    reshape x2, local copies, waits for them, and re-layouts, shards(): left = left.reshape(FEATURES, quadrature, listed, tile // ROWS, ROWS)  5.4 us

profile of v2, /device:TPU:15, one launch (start us, length us, event | category | flops | bytes accessed | tf_op | source)
XLA Modules:
  0.0 207.5 jit_solution(15938164727697566583)
XLA Ops:
  0.0 0.1 pad_add_fusion.7
  0.1 0.8 select_reduce_fusion
  1.0 0.1 add.173
  1.1 0.1 add.176
  1.2 0.1 tile.12
  1.3 0.1 reshape.527
  1.4 0.6 gather_fusion
  2.0 0.6 gather_fusion.1
  2.7 0.2 reduce-window.4
  2.9 0.1 select_reduce_fusion.2
  3.0 0.1 fusion.20
  3.1 0.1 fusion.23
  3.2 0.1 fusion.11
  3.3 0.1 fusion.21
  3.4 0.1 copy.44
  3.5 0.7 reshape.529.own_plan
  4.2 0.7 gather_fusion.2
  4.9 0.7 gather_fusion.3
  5.6 0.1 copy.43
  5.7 0.6 reshape.528.plan
  6.3 0.7 reshape.530
  7.0 1.3 select_maximum_fusion.own
  8.4 19.4 %gather_panels.1 = f32[4,8,24,256]{3,2,1,0:T(8,128)} custom-call(f32[24,256]{1,0:T(8,128)} %select_maximum_fusion.own), custom_call_target="tpu_custom_call" | custom-call | tf_op jit(solution)/shard_map/gather_panels/pallas_call | solution.py:66
  27.8 1.7 gather_fusion.4
  29.5 0.2 fusion.4
  29.8 0.1 div.31
  29.9 0.1 div.30
  30.1 0.7 pad.18.exact
  30.8 0.2 copy_multiply_fusion
  31.0 0.1 copy_multiply_fusion.1
  31.2 0.3 fusion.1
  31.4 2.6 %concatenate.101 = bf16[30,4,8,512]{3,0,1,2:T(8,128)(2,1)S(1)} concatenate(bf16[5,4,8,512]{3,0,1,2:T(8,128)(2,1)S(1)} %get-tuple-element.12, bf16[5,4,8,512]{3,0,1,2:T(8,128)(2,1)S(1)} %get-tuple-element.11, bf16[5,4,8,512]{3,0,1,2:T(8,128)(2,1)S(1)} %get-tuple-element.12, bf16[5,4,8,512]{3,0,1,2:T(8,128)(2,1)S(1)} %get-tuple-element.11, ...), dimensions={0} | concatenate | bytes 1966080 | tf_op jit(solution)/shard_map/concatenate | solution.py:376
  34.0 1.1 pad_bitcast_fusion.right
  35.3 0.1 fusion.5
  35.3 0.1 pad.16
  35.5 1.1 reshape.532
  36.6 4.3 %copy.52 = bf16[32,4,8,8,64]{0,4,1,3,2:T(8,128)(2,1)} copy(bf16[32,4,8,8,64]{4,3,2,1,0:T(8,128)(2,1)S(1)} %reshape.532) | data formatting | bytes 2097152 | tf_op jit(solution)/shard_map/reshape | solution.py:380
  40.9 166.6 %assemble_and_factor.1 = f32[16384,128]{1,0:T(8,128)} custom-call(s32[84]{0:T(128)} %reshape.528.plan, s32[16]{0:T(128)} %reshape.529.own_plan, bf16[8,8,256,32]{3,2,1,0:T(8,128)(2,1)} %bitcast.75, bf16[8,4,32,512]{3,2,1,0:T(8,128)(2,1)} %pad_bitcast_fusion.right, f32[8,8,512]{2,1,0:T(8,128)} %pad.18.exact), custom_call_target="tpu_custom_call" | custom-call | tf_op jit(solution)/shard_map/assemble_and_factor/pallas_call | solution.py:432
  (43 shorter events, 0.5 us)
